TPU v7x, 32 devices: a whole 2x2x4 slice. The times are simulated.
32 devices in a mesh: row: 8 (over z, y), col: 4 (over x, core).
Axes of the slice: x: 2, y: 2, z: 4, core: 2. Of those that a mesh axis runs over, the one named last changes fastest.
Arguments:
- rhs: float32 [2, 4096, 4096], P(None, 'row', 'col'), may hold values from -6 to 6
- factor: float32 [2, 4096, 1024], P(None, 'row', 'col'), may hold values from -0.1875 to 0.1875
- inverses: float32 [2, 512, 512], replicated, may hold values from -1 to 3, as said below
Outputs:
- updated: float32 [2, 4096, 4096], P(None, 'row', 'col')
Inputs may be any that keep to these rules, and one draw needn't show every extreme that they name: `inverses`: each inverse is lower triangular with a diagonal between 0.3 and 3.
All inputs are finite; a program needn't handle non-finite values.
Results may differ from a plain program's by a relative error of at most 0.000064.
Values sent between devices are 32-bit elements; how exact they have to be, the bound alone decides.
A program may use at most 128 MiB of HBM per device.

v0:
```python
import jax
import jax.numpy as jnp
from jax import lax
from jax.sharding import PartitionSpec as P


def broadcast(shard, axis, root):
    mine = lax.axis_index(axis) == root
    return lax.psum(jnp.where(mine, shard, jnp.zeros_like(shard)), axis)


def product(left, right):
    return jnp.dot(left, right, precision=lax.Precision.HIGHEST, preferred_element_type=jnp.float32)


def block_update(panel_part, solved):
    return jnp.einsum("jtk,kc->jtc", panel_part, solved, precision=lax.Precision.HIGHEST)


def shards(rhs, factor, inverses):
    row_index = lax.axis_index("row")
    width = inverses.shape[1]
    panel = lax.all_gather(factor, "col", axis=2, tiled=True)
    coupling_local = panel[0, :, :width]
    first = broadcast(product(inverses[0], rhs[0]), "row", 0)
    leading = rhs[0] - product(coupling_local, first)
    second = broadcast(product(inverses[1], leading), "row", 1)
    after_first = rhs - block_update(panel[..., :width], first)
    result = after_first - block_update(panel[..., width:], second)
    lead_block = jnp.where(row_index == 0, first, jnp.where(row_index == 1, second, result[0]))
    return result.at[0].set(lead_block)


def solution(mesh):
    placed = (P(None, "row", "col"), P(None, "row", "col"), P())
    return jax.shard_map(
        shards, mesh=mesh, in_specs=placed, out_specs=P(None, "row", "col"), check_vma=False
    )
```

profile of v0, /device:TPU:28, one launch (start us, length us, event | category | flops | bytes accessed | tf_op | source)
XLA Modules:
  0.0 251.9 jit_solution(13475776282864391394)
XLA Ops:
  7.4 0.0 all-reduce.3.cloned.1.call-start
  7.4 6.8 %fusion.15 = f32[512,1024]{1,0:T(8,128)} fusion(f32[2,512,1024]{2,1,0:T(8,128)} %param.5, f32[2,512,512]{2,1,0:T(8,128)} %param.7, pred[]{:T(512)S(6)} %eq.8), kind=kOutput, calls=%fused_computation.20 | convolution fusion | flops 3221749760 | bytes 5242881 | tf_op jit(solution)/shard_map/dot_general | solution.py:13
  14.2 0.0 all-reduce.3.cloned.1.call-update
  14.2 0.0 all-gather.2.cloned.1.call-start
  14.2 0.0 copy-start.3
  14.2 0.5 all-gather.2.cloned.1.call-update
  14.8 0.0 all-reduce.5.cloned.1.call-start
  14.8 100.9 %all-reduce.3.cloned.1.call-done = f32[512,1024]{1,0:T(8,128)} async-done(((f32[512,1024]{1,0:T(8,128)}), f32[512,1024]{1,0:T(8,128)}) %all-reduce.3.cloned.1.call-update) | async-done | bytes 2097168 | tf_op jit(solution)/shard_map/psum | solution.py:9
  115.7 0.0 all-gather.2.cloned.1.call-done
  115.7 0.0 copy-start.1
  115.7 5.5 %fusion.18 = f32[1024,512]{0,1:T(8,128)S(1)} fusion(f32[512,1024]{1,0:T(8,128)} %all-reduce.3.cloned.1.call-done, f32[2,512,1024]{2,1,0:T(8,128)} %all-gather.2.cloned.1.call-done), kind=kOutput, calls=%fused_computation.22 | convolution fusion | flops 3221225472 | bytes 5242880 | tf_op jit(solution)/shard_map/dot_general | solution.py:13
  121.3 0.0 copy-done.3
  121.3 0.0 copy-done.1
  121.3 4.9 %select_bitcast_fusion = f32[512,1024]{1,0:T(8,128)} fusion(f32[1024,512]{0,1:T(8,128)S(1)} %fusion.18, f32[2,512,1024]{2,1,0:T(8,128)S(1)} %copy-done.1, f32[2,512,512]{2,1,0:T(8,128)S(1)} %copy-done.3, pred[]{:T(512)S(6)} %eq.9), kind=kOutput, calls=%fused_computation.17 | convolution fusion | flops 3222274048 | bytes 7340033 | tf_op jit(solution)/shard_map/dot_general | solution.py:13
  126.2 0.0 copy-start
  126.2 0.0 all-reduce.5.cloned.1.call-update
  126.2 1.6 copy-done
  127.8 9.6 %fusion.5 = f32[1024,2,512]{0,2,1:T(8,128)} fusion(f32[2,512,1024]{2,1,0:T(8,128)} %all-gather.2.cloned.1.call-done, f32[512,1024]{1,0:T(8,128)S(1)} %copy-done), kind=kOutput, calls=%fused_computation.8 | convolution fusion | flops 6442450944 | bytes 8388608 | tf_op jit(solution)/shard_map/jtk,kc->jtc/dot_general | solution.py:17
  137.4 90.6 %all-reduce.5.cloned.1.call-done = f32[512,1024]{1,0:T(8,128)} async-done(((f32[512,1024]{1,0:T(8,128)}), f32[512,1024]{1,0:T(8,128)}) %all-reduce.5.cloned.1.call-update) | async-done | bytes 2097168 | tf_op jit(solution)/shard_map/psum | solution.py:9
  228.0 0.0 copy-start.2
  228.0 12.8 %bitcast_subtract_fusion = f32[2,512,1024]{2,1,0:T(8,128)} fusion(f32[2,512,1024]{2,1,0:T(8,128)} %param.5, f32[1024,2,512]{0,2,1:T(8,128)} %fusion.5, f32[2,512,1024]{2,1,0:T(8,128)} %all-gather.2.cloned.1.call-done, f32[512,1024]{1,0:T(8,128)} %all-reduce.5.cloned.1.call-done), kind=kOutput, calls=%fused_computation | convolution fusion | flops 6444548096 | bytes 16777216 | tf_op jit(solution)/shard_map/jtk,kc->jtc/dot_general | solution.py:17
  240.8 0.0 copy-done.2
  240.8 3.6 %fusion.3 = f32[2,512,1024]{2,1,0:T(8,128)} fusion(f32[2,512,1024]{2,1,0:T(8,128)} %bitcast_subtract_fusion, f32[512,1024]{1,0:T(8,128)S(1)} %copy-done, f32[512,1024]{1,0:T(8,128)S(1)} %copy-done.2, pred[]{:T(512)S(6)} %eq.9, pred[]{:T(512)S(6)} %eq.8), kind=kLoop, calls=%fused_computation.6 | loop fusion | flops 1048576 | bytes 8388610 | tf_op jit(solution)/shard_map/scatter | solution.py:31
Async XLA Ops:
  7.4 108.4 %all-reduce.3.cloned.1.call-start = ((), (), s32[]{:S(2)}) async-start(), calls=%async_computation | async-start | bytes 4194304 | tf_op jit(solution)/shard_map/psum | solution.py:9
  14.2 101.6 %all-gather.2.cloned.1.call-start = ((), (), s32[]{:S(2)}) async-start(), calls=%async_computation.1 | async-start | bytes 5242880 | tf_op jit(solution)/shard_map/all_gather | solution.py:23
  14.2 107.0 %copy-start.3 = (f32[2,512,512]{2,1,0:T(8,128)S(1)}, f32[2,512,512]{2,1,0:T(8,128)}, u32[]{:S(2)}) copy-start(f32[2,512,512]{2,1,0:T(8,128)} %param.7) | copy-start | bytes 6291460
  14.8 213.2 %all-reduce.5.cloned.1.call-start = ((), (), s32[]{:S(2)}) async-start(), calls=%async_computation.2 | async-start | bytes 4194304 | tf_op jit(solution)/shard_map/psum | solution.py:9
  115.7 5.5 %copy-start.1 = (f32[2,512,1024]{2,1,0:T(8,128)S(1)}, f32[2,512,1024]{2,1,0:T(8,128)}, u32[]{:S(2)}) copy-start(f32[2,512,1024]{2,1,0:T(8,128)} %param.5) | copy-start | bytes 12582916
  126.2 1.6 copy-start
  228.0 12.8 %copy-start.2 = (f32[512,1024]{1,0:T(8,128)S(1)}, f32[512,1024]{1,0:T(8,128)}, u32[]{:S(2)}) copy-start(f32[512,1024]{1,0:T(8,128)} %all-reduce.5.cloned.1.call-done) | copy-start | bytes 6291460
Sparse Core Ops, SparseCore 0:
  14.3 101.3 all-reduce.2
  126.4 101.5 all-reduce.4
Sparse Core Ops, SparseCore 1:
  16.2 35.3 all-gather.1
where the time goes:
time: 255 us; the launch traced here: 252 us
  waiting for transfers between devices  192 us (75%)
  matrix products  39.7 us (16%)
  between operations  14.9 us (6%)
  other arithmetic  3.63 us (1%)
    psum x2, waiting for transfers between devices, broadcast(): return lax.psum(jnp.where(mine, shard, jnp.zeros_like(shard)), axis)  191 us
    dot_general x2, matrix products, block_update(): jnp.einsum('jtk,kc->jtc', panel_part, solved, precision=lax.Precision.HIG...  22.4 us
    dot_general x3, matrix products, product(): jnp.dot(left, right, precision=lax.Precision.HIGHEST, preferred_element_t...  17.2 us
  transfers between devices with their start and end apart: 3, of which 2 were waited for; matrix products, arithmetic and copies ran while one was open for 4% of the time, Pallas kernels for 0%

commit v1 on v0

v1 whole, which is shorter than its diff:
```python
import functools

import jax
import jax.numpy as jnp
from jax import lax
from jax.experimental import pallas as pl
from jax.experimental.pallas import tpu as pltpu
from jax.sharding import PartitionSpec as P

MESH = pl.DeviceIdType.MESH
CW = 256
PR = 64
WINDOW = 4


def split(value):
    high = value.astype(jnp.bfloat16)
    low = (value - high.astype(jnp.float32)).astype(jnp.bfloat16)
    return high, low


def dot3(ah, al, bh, bl):
    def one(a, b):
        return jnp.dot(a, b, preferred_element_type=jnp.float32)

    return one(ah, bh) + one(al, bh) + one(ah, bl)


def kernel(n_row, rhs, fac, inv, out, acc, lane, pan, l10p, invf, ph, plo, ih, il, lh, ll, xh, xl, bh, bl, f32s, s32s,
           acc_sem, inv_sem, own_sem, out_sem, zs, zr, ys, yr, xs, xr, ps, pr, ts, tr, ls, lr):
    nb = rhs.shape[1]
    n_chunk = rhs.shape[2] // CW
    ppc = nb // PR
    n_l = ppc // 2
    n_piece = n_chunk * ppc + n_l
    l_at = 2 * ppc
    half = nb // 2

    r = lax.axis_index("row")
    c = lax.axis_index("col")
    z, y = r // 2, r % 2
    n_z = n_row // 2
    core = c % 2
    partner = c + 1 - 2 * core
    peer = (c + 2) % 4
    peer2 = (partner + 2) % 4
    has_up = z < n_z - 1
    has_down = z > 0
    up, down, across = (r + 2, c), (r - 2, c), (r + 1 - 2 * y, c)
    beside, far = (r, partner), (r, peer)

    def base(k):
        return k * ppc + jnp.where(k >= 2, n_l, 0)

    def load_acc(k, j):
        return pltpu.make_async_copy(
            rhs.at[j, :, pl.ds(k * CW, CW)], acc.at[k, pl.ds(j * nb, nb)], acc_sem.at[k, j])

    for k in range(n_chunk):
        load_acc(k, 0).start()
    own = [pltpu.make_async_copy(fac.at[j], pan.at[c, j], own_sem.at[j]) for j in range(2)]
    inv_copy = [pltpu.make_async_copy(inv.at[i], invf.at[i], inv_sem.at[i]) for i in range(2)]
    for copy in own + inv_copy:
        copy.start()
    for k in range(n_chunk):
        load_acc(k, 1).start()

    barrier = pltpu.get_barrier_semaphore()
    for there in (across, beside, far):
        pl.semaphore_signal(barrier, inc=1, device_id=there, device_id_type=MESH)

    @pl.when(has_up)
    def _():
        pl.semaphore_signal(barrier, inc=1, device_id=up, device_id_type=MESH)

    @pl.when(has_down)
    def _():
        pl.semaphore_signal(barrier, inc=1, device_id=down, device_id_type=MESH)

    pl.semaphore_wait(barrier, 3 + has_up.astype(jnp.int32) + has_down.astype(jnp.int32))

    def remote(src, dst, ssem, rsem, there):
        return pltpu.make_async_remote_copy(
            src_ref=src, dst_ref=dst, send_sem=ssem, recv_sem=rsem, device_id=there, device_id_type=MESH)

    def z_copy(p):
        return remote(lane.at[y, p], lane.at[y, p], zs.at[p], zr.at[p], up)

    def y_copy(p):
        return remote(lane.at[y, p], lane.at[y, p], ys.at[p], yr.at[p], across)

    def y_arrival(p):
        return remote(lane.at[1 - y, p], lane.at[1 - y, p], ys.at[p], yr.at[p], across)

    def x_copy(j):
        return remote(fac.at[j], pan.at[c, j], xs.at[j], xr.at[j], far)

    def x_arrival(j):
        return remote(fac.at[j], pan.at[peer, j], xs.at[j], xr.at[j], far)

    def p_copy(i):
        if i < 2:
            return remote(fac.at[i], pan.at[c, i], ps.at[i], pr.at[i], beside)
        return remote(pan.at[peer, i - 2], pan.at[peer, i - 2], ps.at[i], pr.at[i], beside)

    def p_arrival(i):
        at = partner if i < 2 else peer2
        return remote(pan.at[at, i % 2], pan.at[at, i % 2], ps.at[i], pr.at[i], beside)

    def t_copy(i):
        return remote(pan.at[core, 0, pl.ds(i * PR, PR)], lane.at[0, l_at + i], ts.at[i], tr.at[i], across)

    def l_copy(b):
        return remote(lane.at[b, pl.ds(l_at, n_l)], l10p.at[b], ls.at[b], lr.at[b], beside)

    def relay(p):
        @pl.when(has_down)
        def _():
            z_copy(p).wait_recv()

        @pl.when(jnp.logical_and(z == 0, p >= WINDOW))
        def _():
            y_copy(p - WINDOW).wait_send()

            @pl.when(has_up)
            def _():
                z_copy(p - WINDOW).wait_send()

        @pl.when(has_up)
        def _():
            z_copy(p).start()

        y_copy(p).start()

    def relays(start, stop):
        @pl.loop(start, stop)
        def _(p):
            relay(p)

    def fill(k):
        load_acc(k, 0).wait()

        @pl.when(z == 0)
        def _():
            at = k * ppc + (n_l if k >= 2 else 0)
            lane[y, pl.ds(at, ppc)] = acc[k, pl.ds(0, nb)].reshape(ppc, PR, CW)

    x_copy(0).start()
    p_copy(0).start()
    p_copy(1).start()
    fill(0)
    relays(0, 3)
    for k in range(1, n_chunk):
        fill(k)
    relays(3, 5)
    inv_copy[0].wait()
    ih[0], il[0] = split(invf[0])
    relays(5, 7)
    inv_copy[1].wait()
    ih[1], il[1] = split(invf[1])
    relays(7, 8)

    x_arrival(0).wait_recv()
    p_copy(2).start()
    x_copy(1).start()
    for copy in own:
        copy.wait()

    @pl.when(r == 1)
    def _():
        for i in range(n_l):
            t_copy(i).start()
        lane[1, pl.ds(l_at, n_l)] = pan[core, 0, pl.ds(half, half)].reshape(n_l, PR, CW)

    relays(8, 12)
    p_arrival(0).wait_recv()
    p_arrival(1).wait_recv()
    p_arrival(2).wait_recv()

    def split_panel(q, j):
        h, l = split(pan[q, j])
        ph[pl.ds(j * nb, nb), pl.ds(q * CW, CW)] = h
        plo[pl.ds(j * nb, nb), pl.ds(q * CW, CW)] = l

    for q in range(4):
        relay(12 + q)
        split_panel(q, 0)

    @pl.when(r == 0)
    def _():
        for i in range(n_l):
            t_copy(i).wait_recv()

    relays(16, 18)
    x_arrival(1).wait_recv()
    p_copy(3).start()
    relays(18, 21)
    for i in range(n_l):
        y_arrival(l_at + i).wait_recv()
    for b in range(2):
        l_copy(b).start()
    p_arrival(3).wait_recv()
    for q in range(4):
        if q:
            relay(20 + q)
        split_panel(q, 1)
    for b in range(2):
        l_copy(b).wait_recv()
        for at, block in ((core, lane[b, pl.ds(l_at, n_l)]), (1 - core, l10p[b])):
            h, l = split(block.reshape(half, CW))
            lh[at, pl.ds(b * half, half)] = h
            ll[at, pl.ds(b * half, half)] = l
    for k in range(n_chunk):
        load_acc(k, 1).wait()

    def triangle(i, m):
        rows, cols = slice(m * half, (m + 1) * half), slice(0, (m + 1) * half)
        return dot3(ih[i, rows, cols], il[i, rows, cols], bh[cols], bl[cols])

    def solve(k):
        @pl.loop(base(k), base(k) + ppc)
        def _(p):
            y_arrival(p).wait_recv()

        bh[...], bl[...] = split(lane[0, pl.ds(base(k), ppc)].reshape(nb, CW))
        for m in range(2):
            rows = slice(m * half, (m + 1) * half)
            part = triangle(0, m)
            f32s[rows] = part
            xh[rows], xl[rows] = split(part)
        for m in range(2):
            rows = slice(m * half, (m + 1) * half)
            b1 = lane[1, pl.ds(base(k) + m * n_l, n_l)].reshape(half, CW)
            part = b1
            for q in range(2):
                ks = slice(q * half, (q + 1) * half)
                part = part - dot3(lh[q, rows], ll[q, rows], xh[ks], xl[ks])
            bh[rows], bl[rows] = split(part)
        for m in range(2):
            rows = slice(m * half, (m + 1) * half)
            at = slice(nb + m * half, nb + (m + 1) * half)
            part = triangle(1, m)
            s32s[rows] = part
            xh[at], xl[at] = split(part)

    def out_copy(k, t):
        return pltpu.make_async_copy(
            acc.at[k, pl.ds(pl.multiple_of(t * half, half), half)],
            out.at[t // 2, pl.ds(pl.multiple_of((t % 2) * half, half), half),
                   pl.ds(pl.multiple_of(k * CW, CW), CW)],
            out_sem.at[k, t])

    def update(k, t):
        rows = pl.ds(pl.multiple_of(t * half, half), half)
        solved = jnp.logical_and(r < 2, t < 2)

        @pl.when(jnp.logical_not(solved))
        def _():
            acc[k, rows] = acc[k, rows] - dot3(ph[rows], plo[rows], xh[...], xl[...])

        @pl.when(jnp.logical_and(solved, r == 0))
        def _():
            acc[k, rows] = f32s[rows]

        @pl.when(jnp.logical_and(solved, r == 1))
        def _():
            acc[k, rows] = s32s[rows]

        out_copy(k, t).start()

    def substep(n):
        k, u = n // 5, n % 5

        @pl.when(u == 0)
        def _():
            solve(k)

        @pl.when(u > 0)
        def _():
            update(k, u - 1)

    lead = 5 * (n_chunk - 1)

    @pl.loop(0, 20)
    def _(n):
        @pl.when(jnp.logical_and(n < 16, n % 2 == 0))
        def _():
            relay(24 + n // 2)

        @pl.when(n == lead)
        def _():
            relays(32, n_piece)

        substep(n)

    x_copy(0).wait_send()
    x_copy(1).wait_send()
    for i in range(4):
        p_copy(i).wait_send()
    for b in range(2):
        l_copy(b).wait_send()

    @pl.when(r == 1)
    def _():
        for i in range(n_l):
            t_copy(i).wait_send()

    @pl.loop(jnp.where(z == 0, n_piece - WINDOW, 0), n_piece)
    def _(p):
        y_copy(p).wait_send()

        @pl.when(has_up)
        def _():
            z_copy(p).wait_send()

    @pl.loop(0, n_chunk)
    def _(k):
        for t in range(4):
            out_copy(k, t).wait()


def shards(n_row, rhs, factor, inverses):
    nb = rhs.shape[1]
    n_chunk = rhs.shape[2] // CW
    ppc = nb // PR
    n_l = ppc // 2
    n_piece = n_chunk * ppc + n_l
    f32, bf16, dma = jnp.float32, jnp.bfloat16, pltpu.SemaphoreType.DMA
    anywhere = pl.BlockSpec(memory_space=pl.ANY)
    return pl.pallas_call(
        functools.partial(kernel, n_row),
        out_shape=jax.ShapeDtypeStruct(rhs.shape, f32),
        in_specs=[anywhere] * 3,
        out_specs=anywhere,
        scratch_shapes=[
            pltpu.VMEM((n_chunk, 2 * nb, CW), f32),
            pltpu.VMEM((2, n_piece, PR, CW), f32),
            pltpu.VMEM((4, 2, nb, CW), f32),
            pltpu.VMEM((2, n_l, PR, CW), f32),
            pltpu.VMEM((2, nb, nb), f32),
            pltpu.VMEM((2 * nb, 2 * nb), bf16),
            pltpu.VMEM((2 * nb, 2 * nb), bf16),
            pltpu.VMEM((2, nb, nb), bf16),
            pltpu.VMEM((2, nb, nb), bf16),
            pltpu.VMEM((2, nb, CW), bf16),
            pltpu.VMEM((2, nb, CW), bf16),
            pltpu.VMEM((2 * nb, CW), bf16),
            pltpu.VMEM((2 * nb, CW), bf16),
            pltpu.VMEM((nb, CW), bf16),
            pltpu.VMEM((nb, CW), bf16),
            pltpu.VMEM((nb, CW), f32),
            pltpu.VMEM((nb, CW), f32),
            dma((n_chunk, 2)), dma((2,)), dma((2,)), dma((n_chunk, 4)),
            dma((n_piece,)), dma((n_piece,)), dma((n_piece,)), dma((n_piece,)),
            dma((2,)), dma((2,)), dma((4,)), dma((4,)),
            dma((n_l,)), dma((n_l,)), dma((2,)), dma((2,)),
        ],
        compiler_params=pltpu.CompilerParams(
            collective_id=0, has_side_effects=True, vmem_limit_bytes=56 * 1024 * 1024),
        cost_estimate=pl.CostEstimate(flops=8 * 10 ** 9, bytes_accessed=12 * 2 ** 20, transcendentals=0),
    )(rhs, factor, inverses)


def solution(mesh):
    placed = (P(None, "row", "col"), P(None, "row", "col"), P())
    return jax.shard_map(
        functools.partial(shards, mesh.shape["row"]), mesh=mesh, in_specs=placed,
        out_specs=P(None, "row", "col"), check_vma=False)
```

time: 255 us -> 85.5 us (0.34)
  waiting for transfers between devices: 192 us -> 0 us
  Pallas kernels: 0 us -> 80 us
  matrix products: 39.7 us -> 0 us
  between operations: 14.9 us -> 0.01 us
  other arithmetic: 3.63 us -> 0 us
  local copies, waits for them, and re-layouts: 1.58 us -> 4.79 us
    psum x2 -> x0, waiting for transfers between devices: 191 us -> none  [broadcast(): return lax.psum(jnp.where(mine, shard, jnp.zeros_like(shard)), axis)]
    pallas_call x0 -> x1, Pallas kernels: none -> 80 us  [shards(): pl.pallas_call(functools.partial(kernel, n_row), out_shape=jax.ShapeDtype...]
    dot_general x5 -> x0, matrix products: 39.7 us -> none  [the longest x2 22.4 us: block_update(): jnp.einsum('jtk,kc->jtc', panel_part, solved, precision=lax.Precision.HIG...]
    scatter x1 -> x0, other arithmetic: 3.63 us -> none  [shards(): return result.at[0].set(lead_block)]
    unnamed x8 -> x1, local copies, waits for them, and re-layouts: 1.58 us -> 4.79 us
  transfers between devices with their start and end apart: 3 -> 0, of which waited for: 2 -> 0; matrix products, arithmetic and copies ran while one was open for 4% -> 0% of each run, Pallas kernels for 0% -> 0%
where the time goes in v1:
time: 85.5 us; the launch traced here: 84.8 us
  Pallas kernels  80 us (94%)
  local copies, waits for them, and re-layouts  4.79 us (6%)
    pallas_call x1, Pallas kernels, shards(): pl.pallas_call(functools.partial(kernel, n_row), out_shape=jax.ShapeDtype...  80 us
    unnamed x1, local copies, waits for them, and re-layouts  4.79 us

profile of v1, /device:TPU:28, one launch (start us, length us, event | category | flops | bytes accessed | tf_op | source)
XLA Modules:
  0.0 84.8 jit_solution(12841041933058667527)
XLA Ops:
  0.0 80.0 %shard_map.37 = f32[2,512,1024]{2,1,0:T(8,128)} custom-call(f32[2,512,1024]{2,1,0:T(8,128)} %rhs.1, f32[2,512,256]{2,1,0:T(8,128)} %fac.1, f32[2,512,512]{2,1,0:T(8,128)} %inv.1), custom_call_target="tpu_custom_call" | custom-call | flops 8000000000 | bytes 12582912 | tf_op jit(solution)/shard_map/pallas_call | solution.py:330
  80.0 4.8 %copy.5 = f32[2,512,1024]{2,1,0:T(8,128)} copy(f32[2,512,1024]{2,1,0:T(8,128)} %shard_map.37) | data formatting | bytes 8388608

commit v2 on v1

v2 whole, which is shorter than its diff:
```python
import functools

import jax
import jax.numpy as jnp
from jax import lax
from jax.experimental import pallas as pl
from jax.experimental.pallas import tpu as pltpu
from jax.sharding import PartitionSpec as P

MESH = pl.DeviceIdType.MESH
CW = 256
PR = 32
WINDOW = 10


def split(value):
    high = value.astype(jnp.bfloat16)
    low = (value - high.astype(jnp.float32)).astype(jnp.bfloat16)
    return high, low


def dot3(ah, al, bh, bl):
    def one(a, b):
        return jnp.dot(a, b, preferred_element_type=jnp.float32)

    return one(ah, bh) + one(al, bh) + one(ah, bl)


def kernel(n_row, rhs, fac, inv, out, lane, pan, l10p, invf, mh, ml, ih, il, lh, ll, xh, xl,
           acc_sem, inv_sem, own_sem, zs, zr, ys, yr, xs, xr, ps, pr, ts, tr, ls, lr):
    nb = rhs.shape[1]
    n_chunk = rhs.shape[2] // CW
    ppc = nb // PR
    n_l = ppc // 2
    n_piece = n_chunk * ppc + n_l
    l_at = 2 * ppc
    half = nb // 2

    r = lax.axis_index("row")
    c = lax.axis_index("col")
    z, y = r // 2, r % 2
    n_z = n_row // 2
    core = c % 2
    partner = c + 1 - 2 * core
    peer = (c + 2) % 4
    peer2 = (partner + 2) % 4
    has_up = z < n_z - 1
    has_down = z > 0
    up, down, across = (r + 2, c), (r - 2, c), (r + 1 - 2 * y, c)
    beside, far = (r, partner), (r, peer)

    def load_lead(k):
        cols = pl.ds(k * CW, CW)
        return pltpu.make_async_copy(rhs.at[0, :, cols], out.at[0, :, cols], acc_sem.at[k])

    load_rest = pltpu.make_async_copy(rhs.at[1], out.at[1], acc_sem.at[n_chunk])
    own = [pltpu.make_async_copy(fac.at[j], pan.at[c, j], own_sem.at[j]) for j in range(2)]
    inv_copy = [pltpu.make_async_copy(inv.at[i], invf.at[i], inv_sem.at[i]) for i in range(2)]
    for k in range(n_chunk):
        load_lead(k).start()
    for copy in own + inv_copy + [load_rest]:
        copy.start()

    barrier = pltpu.get_barrier_semaphore()
    for there in (across, beside, far):
        pl.semaphore_signal(barrier, inc=1, device_id=there, device_id_type=MESH)

    @pl.when(has_up)
    def _():
        pl.semaphore_signal(barrier, inc=1, device_id=up, device_id_type=MESH)

    @pl.when(has_down)
    def _():
        pl.semaphore_signal(barrier, inc=1, device_id=down, device_id_type=MESH)

    def fill(k):
        load_lead(k).wait()

        @pl.when(z == 0)
        def _():
            at = k * ppc + (n_l if k >= 2 else 0)
            lane[y, pl.ds(at, ppc)] = out[0, :, k * CW:(k + 1) * CW].reshape(ppc, PR, CW)

    fill(0)
    pl.semaphore_wait(barrier, 3 + has_up.astype(jnp.int32) + has_down.astype(jnp.int32))

    def remote(src, dst, ssem, rsem, there):
        return pltpu.make_async_remote_copy(
            src_ref=src, dst_ref=dst, send_sem=ssem, recv_sem=rsem, device_id=there, device_id_type=MESH)

    def z_copy(p):
        return remote(lane.at[y, p], lane.at[y, p], zs.at[p], zr.at[p], up)

    def y_copy(p):
        return remote(lane.at[y, p], lane.at[y, p], ys.at[p], yr.at[p], across)

    def y_arrival(p):
        return remote(lane.at[1 - y, p], lane.at[1 - y, p], ys.at[p], yr.at[p], across)

    def x_copy(j):
        return remote(fac.at[j], pan.at[c, j], xs.at[j], xr.at[j], far)

    def x_arrival(j):
        return remote(fac.at[j], pan.at[peer, j], xs.at[j], xr.at[j], far)

    def p_copy(i):
        if i < 2:
            return remote(fac.at[i], pan.at[c, i], ps.at[i], pr.at[i], beside)
        return remote(pan.at[peer, i - 2], pan.at[peer, i - 2], ps.at[i], pr.at[i], beside)

    def p_arrival(i):
        at = partner if i < 2 else peer2
        return remote(pan.at[at, i % 2], pan.at[at, i % 2], ps.at[i], pr.at[i], beside)

    def t_copy(i):
        return remote(pan.at[core, 0, pl.ds(i * PR, PR)], lane.at[0, l_at + i], ts.at[i], tr.at[i], across)

    def l_copy(b):
        return remote(lane.at[b, pl.ds(l_at, n_l)], l10p.at[b], ls.at[b], lr.at[b], beside)

    def relay(p):
        @pl.when(has_down)
        def _():
            z_copy(p).wait_recv()

        @pl.when(jnp.logical_and(z == 0, p >= WINDOW))
        def _():
            y_copy(p - WINDOW).wait_send()

            @pl.when(has_up)
            def _():
                z_copy(p - WINDOW).wait_send()

        @pl.when(has_up)
        def _():
            z_copy(p).start()

        y_copy(p).start()

    def relays(start, stop):
        @pl.loop(start, stop)
        def _(p):
            relay(p)

    x_copy(0).start()
    p_copy(0).start()
    p_copy(1).start()
    relays(0, 4)
    for k in range(1, n_chunk):
        fill(k)
        relay(3 + k)

    @pl.when(r < 2)
    def _():
        out[0] = jnp.zeros_like(out[0])

    relays(7, 9)
    for i in range(2):
        inv_copy[i].wait()
        for h in range(2):
            rows = slice(h * half, (h + 1) * half)
            ih[i, rows], il[i, rows] = split(invf[i, rows])
            relay(9 + 2 * i + h)
    relays(13, 18)

    x_arrival(0).wait_recv()
    p_copy(2).start()
    x_copy(1).start()
    for copy in own:
        copy.wait()

    @pl.when(r == 1)
    def _():
        for i in range(n_l):
            t_copy(i).start()
        lane[1, pl.ds(l_at, n_l)] = pan[core, 0, pl.ds(half, half)].reshape(n_l, PR, CW)

    relays(18, 25)
    for i in range(3):
        p_arrival(i).wait_recv()

    at_row = lax.broadcasted_iota(jnp.int32, (half, CW), 0)
    at_col = lax.broadcasted_iota(jnp.int32, (half, CW), 1)
    minus_one = jnp.where(at_row == at_col, -1.0, 0.0).astype(jnp.float32)

    def panel(q, t):
        j, m = t // 2, t % 2
        value = pan[q, j, m * half:(m + 1) * half]
        if j:
            return value
        mine = minus_one if q % 2 == m else jnp.zeros_like(minus_one)
        solved = jnp.where(r == q // 2, mine, jnp.zeros_like(mine))
        return jnp.where(r < 2, solved, value)

    def triangle(i, parts):
        (ah, al), (bh, bl) = parts
        first = (dot3(ah, al, ih[i, :half, :half], il[i, :half, :half])
                 + dot3(bh, bl, ih[i, half:, :half], il[i, half:, :half]))
        return first, dot3(bh, bl, ih[i, half:, half:], il[i, half:, half:])

    def keep(t, b, products):
        rows = slice(t * half, (t + 1) * half)
        for h, value in enumerate(products):
            at = slice((2 * h + b) * CW, (2 * h + b + 1) * CW)
            mh[rows, at], ml[rows, at] = split(value)

    def second_factor(t):
        keep(t, 1, triangle(1, [split(panel(2, t)), split(panel(3, t))]))

    def first_factor(t):
        rows = slice(t * half, (t + 1) * half)
        parts = []
        for q in range(2):
            value = panel(q, t)
            for h in range(2):
                at = slice((2 * h + 1) * CW, (2 * h + 2) * CW)
                ks = slice(h * half, (h + 1) * half)
                value = value - dot3(mh[rows, at], ml[rows, at], lh[q, ks], ll[q, ks])
            parts.append(split(value))
        keep(t, 0, triangle(0, parts))

    second_factor(0)
    relays(25, 27)
    second_factor(1)
    relays(27, 32)

    @pl.when(r == 0)
    def _():
        for i in range(n_l):
            t_copy(i).wait_recv()

    relays(32, 38)
    x_arrival(1).wait_recv()
    p_copy(3).start()
    relays(38, 42)
    for i in range(n_l):
        y_arrival(l_at + i).wait_recv()
    for b in range(2):
        l_copy(b).start()
    relay(42)
    p_arrival(3).wait_recv()
    second_factor(2)
    relay(43)
    second_factor(3)
    relay(44)
    for b in range(2):
        l_copy(b).wait_recv()
        for at, block in ((core, lane[b, pl.ds(l_at, n_l)]), (1 - core, l10p[b])):
            h, l = split(block.reshape(half, CW))
            lh[at, pl.ds(b * half, half)] = h
            ll[at, pl.ds(b * half, half)] = l
    load_rest.wait()
    for t in range(4):
        relay(45 + 2 * t)
        first_factor(t)
        relay(46 + 2 * t)

    def gather(g):
        k, h = g // 2, g % 2
        start = k * ppc + jnp.where(k >= 2, n_l, 0) + h * n_l

        @pl.loop(start, start + n_l)
        def _(p):
            y_arrival(p).wait_recv()

        for b in range(2):
            rows = slice(b * half, (b + 1) * half)
            xh[rows], xl[rows] = split(lane[b, pl.ds(start, n_l)].reshape(half, CW))

    def update(g, t):
        k, h = g // 2, g % 2
        rows = pl.ds(pl.multiple_of(t * half, half), half)
        place = (t // 2, pl.ds(pl.multiple_of((t % 2) * half, half), half), pl.ds(pl.multiple_of(k * CW, CW), CW))
        ks = pl.ds(pl.multiple_of(h * 2 * CW, 2 * CW), 2 * CW)
        out[place] = out[place] - dot3(mh[rows, ks], ml[rows, ks], xh[...], xl[...])

    @pl.loop(0, 4 * 2 * n_chunk)
    def _(n):
        g, t = n // 4, n % 4

        @pl.when(jnp.logical_and(g < 6, t < 3))
        def _():
            relay(53 + 3 * g + t)

        @pl.when(n == 24)
        def _():
            relays(71, n_piece)

        @pl.when(t == 0)
        def _():
            gather(g)

        update(g, t)

    x_copy(0).wait_send()
    x_copy(1).wait_send()
    for i in range(4):
        p_copy(i).wait_send()
    for b in range(2):
        l_copy(b).wait_send()

    @pl.when(r == 1)
    def _():
        for i in range(n_l):
            t_copy(i).wait_send()

    @pl.loop(jnp.where(z == 0, n_piece - WINDOW, 0), n_piece)
    def _(p):
        y_copy(p).wait_send()

        @pl.when(has_up)
        def _():
            z_copy(p).wait_send()


def shards(n_row, rhs, factor, inverses):
    nb = rhs.shape[1]
    n_chunk = rhs.shape[2] // CW
    ppc = nb // PR
    n_l = ppc // 2
    n_piece = n_chunk * ppc + n_l
    f32, bf16, dma = jnp.float32, jnp.bfloat16, pltpu.SemaphoreType.DMA
    anywhere = pl.BlockSpec(memory_space=pl.ANY)
    return pl.pallas_call(
        functools.partial(kernel, n_row),
        out_shape=pltpu.VMEM(rhs.shape, f32),
        in_specs=[anywhere] * 3,
        out_specs=pl.BlockSpec(memory_space=pltpu.VMEM),
        scratch_shapes=[
            pltpu.VMEM((2, n_piece, PR, CW), f32),
            pltpu.VMEM((4, 2, nb, CW), f32),
            pltpu.VMEM((2, n_l, PR, CW), f32),
            pltpu.VMEM((2, nb, nb), f32),
            pltpu.VMEM((2 * nb, 2 * nb), bf16),
            pltpu.VMEM((2 * nb, 2 * nb), bf16),
            pltpu.VMEM((2, nb, nb), bf16),
            pltpu.VMEM((2, nb, nb), bf16),
            pltpu.VMEM((2, nb, CW), bf16),
            pltpu.VMEM((2, nb, CW), bf16),
            pltpu.VMEM((nb, CW), bf16),
            pltpu.VMEM((nb, CW), bf16),
            dma((n_chunk + 1,)), dma((2,)), dma((2,)),
            dma((n_piece,)), dma((n_piece,)), dma((n_piece,)), dma((n_piece,)),
            dma((2,)), dma((2,)), dma((4,)), dma((4,)),
            dma((n_l,)), dma((n_l,)), dma((2,)), dma((2,)),
        ],
        compiler_params=pltpu.CompilerParams(
            collective_id=0, has_side_effects=True, vmem_limit_bytes=59 * 1024 * 1024),
        cost_estimate=pl.CostEstimate(flops=8 * 10 ** 9, bytes_accessed=12 * 2 ** 20, transcendentals=0),
    )(rhs, factor, inverses)


def solution(mesh):
    placed = (P(None, "row", "col"), P(None, "row", "col"), P())
    return jax.shard_map(
        functools.partial(shards, mesh.shape["row"]), mesh=mesh, in_specs=placed,
        out_specs=P(None, "row", "col"), check_vma=False)
```

time: 85.5 us -> 76.7 us (0.90)
  Pallas kernels: 80 us -> 74.5 us
  local copies, waits for them, and re-layouts: 4.79 us -> 2.02 us
    pallas_call x1, Pallas kernels: 80 us -> 74.5 us  [shards(): pl.pallas_call(functools.partial(kernel, n_row), out_shape=pltpu.VMEM(rhs...]
    unnamed x1, local copies, waits for them, and re-layouts: 4.79 us -> 2.02 us
where the time goes in v2:
time: 76.7 us; the launch traced here: 76.5 us
  Pallas kernels  74.5 us (97%)
  local copies, waits for them, and re-layouts  2.02 us (3%)
    pallas_call x1, Pallas kernels, shards(): pl.pallas_call(functools.partial(kernel, n_row), out_shape=pltpu.VMEM(rhs...  74.5 us
    unnamed x1, local copies, waits for them, and re-layouts  2.02 us

profile of v2, /device:TPU:28, one launch (start us, length us, event | category | flops | bytes accessed | tf_op | source)
XLA Modules:
  0.0 76.5 jit_solution(5616452440370953513)
XLA Ops:
  0.0 74.5 %shard_map.37 = f32[2,512,1024]{2,1,0:T(8,128)S(1)} custom-call(f32[2,512,1024]{2,1,0:T(8,128)} %rhs.1, f32[2,512,256]{2,1,0:T(8,128)} %fac.1, f32[2,512,512]{2,1,0:T(8,128)} %inv.1), custom_call_target="tpu_custom_call" | custom-call | flops 8000000000 | bytes 12582912 | tf_op jit(solution)/shard_map/pallas_call | solution.py:324
  74.5 2.0 %copy.5 = f32[2,512,1024]{2,1,0:T(8,128)} copy(f32[2,512,1024]{2,1,0:T(8,128)S(1)} %shard_map.37) | data formatting | bytes 8388608

commit v3 on v2

--- a/solution.py
+++ b/solution.py
@@ -161,11 +161,11 @@
             rows = slice(h * half, (h + 1) * half)
             ih[i, rows], il[i, rows] = split(invf[i, rows])
             relay(9 + 2 * i + h)
+    x_copy(1).start()
     relays(13, 18)
 
     x_arrival(0).wait_recv()
     p_copy(2).start()
-    x_copy(1).start()
     for copy in own:
         copy.wait()
 
@@ -229,20 +229,20 @@
         for i in range(n_l):
             t_copy(i).wait_recv()
 
-    relays(32, 38)
+    relays(32, 41)
     x_arrival(1).wait_recv()
     p_copy(3).start()
-    relays(38, 42)
+    relays(41, 43)
     for i in range(n_l):
         y_arrival(l_at + i).wait_recv()
     for b in range(2):
         l_copy(b).start()
-    relay(42)
+    relays(43, 45)
     p_arrival(3).wait_recv()
     second_factor(2)
-    relay(43)
+    relay(45)
     second_factor(3)
-    relay(44)
+    relays(46, 49)
     for b in range(2):
         l_copy(b).wait_recv()
         for at, block in ((core, lane[b, pl.ds(l_at, n_l)]), (1 - core, l10p[b])):
@@ -251,9 +251,8 @@
             ll[at, pl.ds(b * half, half)] = l
     load_rest.wait()
     for t in range(4):
-        relay(45 + 2 * t)
+        relay(49 + t)
         first_factor(t)
-        relay(46 + 2 * t)
 
     def gather(g):
         k, h = g // 2, g % 2

time: 76.7 us -> 76.7 us (level)
  no operation moved by 1% of the time
where the time goes in v3:
time: 76.7 us; the launch traced here: 76.6 us
  Pallas kernels  74.5 us (97%)
  local copies, waits for them, and re-layouts  2.02 us (3%)
    pallas_call x1, Pallas kernels, shards(): pl.pallas_call(functools.partial(kernel, n_row), out_shape=pltpu.VMEM(rhs...  74.5 us
    unnamed x1, local copies, waits for them, and re-layouts  2.02 us

profile of v3, /device:TPU:28, one launch (start us, length us, event | category | flops | bytes accessed | tf_op | source)
XLA Modules:
  0.0 76.6 jit_solution(17266221117993999043)
XLA Ops:
  0.0 74.5 %shard_map.37 = f32[2,512,1024]{2,1,0:T(8,128)S(1)} custom-call(f32[2,512,1024]{2,1,0:T(8,128)} %rhs.1, f32[2,512,256]{2,1,0:T(8,128)} %fac.1, f32[2,512,512]{2,1,0:T(8,128)} %inv.1), custom_call_target="tpu_custom_call" | custom-call | flops 8000000000 | bytes 12582912 | tf_op jit(solution)/shard_map/pallas_call | solution.py:323
  74.6 2.0 %copy.5 = f32[2,512,1024]{2,1,0:T(8,128)} copy(f32[2,512,1024]{2,1,0:T(8,128)S(1)} %shard_map.37) | data formatting | bytes 8388608

commit v4 on v2

--- a/solution.py
+++ b/solution.py
@@ -10,7 +10,8 @@
 MESH = pl.DeviceIdType.MESH
 CW = 256
 PR = 32
-WINDOW = 10
+Z_WINDOW = 16
+Y_WINDOW = 28
 
 
 def split(value):
@@ -26,21 +27,22 @@
     return one(ah, bh) + one(al, bh) + one(ah, bl)
 
 
-def kernel(n_row, rhs, fac, inv, out, lane, pan, l10p, invf, mh, ml, ih, il, lh, ll, xh, xl,
-           acc_sem, inv_sem, own_sem, zs, zr, ys, yr, xs, xr, ps, pr, ts, tr, ls, lr):
+def kernel(n_row, rhs, fac, inv, out, lane, pan, l10p, l10x, invf, mh, ml, ih, il, lh, ll, xh, xl,
+           acc_sem, inv_sem, own_sem, zs, zr, ys, yr, xs, xr, ps, pr, ts, tr, ls, lr, us, ur):
     nb = rhs.shape[1]
     n_chunk = rhs.shape[2] // CW
     ppc = nb // PR
-    n_l = ppc // 2
+    n_h = ppc // 2
+    n_l = ppc // 4
     n_piece = n_chunk * ppc + n_l
-    l_at = 2 * ppc
-    half = nb // 2
+    l_at = 3 * n_h
+    half, quarter = nb // 2, nb // 4
 
     r = lax.axis_index("row")
     c = lax.axis_index("col")
     z, y = r // 2, r % 2
     n_z = n_row // 2
-    core = c % 2
+    core, x = c % 2, c // 2
     partner = c + 1 - 2 * core
     peer = (c + 2) % 4
     peer2 = (partner + 2) % 4
@@ -73,13 +75,17 @@
     def _():
         pl.semaphore_signal(barrier, inc=1, device_id=down, device_id_type=MESH)
 
+    def first_piece(g):
+        return g * n_h + (n_l if g >= 3 else 0)
+
     def fill(k):
         load_lead(k).wait()
 
         @pl.when(z == 0)
         def _():
-            at = k * ppc + (n_l if k >= 2 else 0)
-            lane[y, pl.ds(at, ppc)] = out[0, :, k * CW:(k + 1) * CW].reshape(ppc, PR, CW)
+            for h in range(2):
+                block = out[0, h * half:(h + 1) * half, k * CW:(k + 1) * CW]
+                lane[y, pl.ds(first_piece(2 * k + h), n_h)] = block.reshape(n_h, PR, CW)
 
     fill(0)
     pl.semaphore_wait(barrier, 3 + has_up.astype(jnp.int32) + has_down.astype(jnp.int32))
@@ -97,11 +103,17 @@
     def y_arrival(p):
         return remote(lane.at[1 - y, p], lane.at[1 - y, p], ys.at[p], yr.at[p], across)
 
-    def x_copy(j):
-        return remote(fac.at[j], pan.at[c, j], xs.at[j], xr.at[j], far)
-
-    def x_arrival(j):
-        return remote(fac.at[j], pan.at[peer, j], xs.at[j], xr.at[j], far)
+    def x_ref(ref, at, i):
+        part = ref.at[0] if i < 4 else ref.at[1]
+        if at is not None:
+            part = ref.at[at, 0] if i < 4 else ref.at[at, 1]
+        return part.at[pl.ds((1, 3, 0, 2)[i] * quarter, quarter)] if i < 4 else part
+
+    def x_copy(i):
+        return remote(x_ref(fac, None, i), x_ref(pan, c, i), xs.at[i], xr.at[i], far)
+
+    def x_arrival(i):
+        return remote(x_ref(fac, None, i), x_ref(pan, peer, i), xs.at[i], xr.at[i], far)
 
     def p_copy(i):
         if i < 2:
@@ -113,27 +125,32 @@
         return remote(pan.at[at, i % 2], pan.at[at, i % 2], ps.at[i], pr.at[i], beside)
 
     def t_copy(i):
-        return remote(pan.at[core, 0, pl.ds(i * PR, PR)], lane.at[0, l_at + i], ts.at[i], tr.at[i], across)
-
-    def l_copy(b):
-        return remote(lane.at[b, pl.ds(l_at, n_l)], l10p.at[b], ls.at[b], lr.at[b], beside)
+        rows = pl.ds(pl.multiple_of(x * quarter + i * PR, PR), PR)
+        return remote(pan.at[core, 0, rows], lane.at[0, l_at + i], ts.at[i], tr.at[i], across)
+
+    def lx_copy(b):
+        return remote(lane.at[b, pl.ds(l_at, n_l)], l10x.at[b], us.at[b], ur.at[b], far)
+
+    def lp_copy(i, b):
+        src = l10x.at[b] if i else lane.at[b, pl.ds(l_at, n_l)]
+        return remote(src, l10p.at[i, b], ls.at[i, b], lr.at[i, b], beside)
 
     def relay(p):
         @pl.when(has_down)
         def _():
             z_copy(p).wait_recv()
 
-        @pl.when(jnp.logical_and(z == 0, p >= WINDOW))
-        def _():
-            y_copy(p - WINDOW).wait_send()
-
-            @pl.when(has_up)
-            def _():
-                z_copy(p - WINDOW).wait_send()
+        @pl.when(jnp.logical_and(jnp.logical_and(z == 0, has_up), p >= Z_WINDOW))
+        def _():
+            z_copy(p - Z_WINDOW).wait_send()
 
         @pl.when(has_up)
         def _():
             z_copy(p).start()
+
+        @pl.when(jnp.logical_and(z == 0, p >= Y_WINDOW))
+        def _():
+            y_copy(p - Y_WINDOW).wait_send()
 
         y_copy(p).start()
 
@@ -143,6 +160,7 @@
             relay(p)
 
     x_copy(0).start()
+    x_copy(1).start()
     p_copy(0).start()
     p_copy(1).start()
     relays(0, 4)
@@ -154,28 +172,42 @@
     def _():
         out[0] = jnp.zeros_like(out[0])
 
-    relays(7, 9)
+    relay(7)
+    x_copy(2).start()
+    x_copy(3).start()
     for i in range(2):
         inv_copy[i].wait()
         for h in range(2):
             rows = slice(h * half, (h + 1) * half)
             ih[i, rows], il[i, rows] = split(invf[i, rows])
-            relay(9 + 2 * i + h)
-    relays(13, 18)
-
-    x_arrival(0).wait_recv()
+            relay(8 + 2 * i + h)
+        if i == 0:
+            x_arrival(0).wait_recv()
+            x_arrival(1).wait_recv()
+            for copy in own:
+                copy.wait()
+
+            @pl.when(r == 1)
+            def _():
+                for e in range(n_l):
+                    t_copy(e).start()
+                rows = pl.ds(pl.multiple_of(half + x * quarter, quarter), quarter)
+                lane[1, pl.ds(l_at, n_l)] = pan[core, 0, rows].reshape(n_l, PR, CW)
+
+    relays(12, 16)
+    x_copy(4).start()
+    relays(16, 19)
+    x_arrival(2).wait_recv()
+    x_arrival(3).wait_recv()
     p_copy(2).start()
-    x_copy(1).start()
-    for copy in own:
-        copy.wait()
-
-    @pl.when(r == 1)
+    relays(19, 24)
+
+    @pl.when(r == 0)
     def _():
         for i in range(n_l):
-            t_copy(i).start()
-        lane[1, pl.ds(l_at, n_l)] = pan[core, 0, pl.ds(half, half)].reshape(n_l, PR, CW)
-
-    relays(18, 25)
+            t_copy(i).wait_recv()
+
+    relays(24, 26)
     for i in range(3):
         p_arrival(i).wait_recv()
 
@@ -220,52 +252,51 @@
         keep(t, 0, triangle(0, parts))
 
     second_factor(0)
-    relays(25, 27)
+    relay(26)
     second_factor(1)
     relays(27, 32)
-
-    @pl.when(r == 0)
-    def _():
-        for i in range(n_l):
-            t_copy(i).wait_recv()
-
-    relays(32, 38)
-    x_arrival(1).wait_recv()
-    p_copy(3).start()
-    relays(38, 42)
     for i in range(n_l):
         y_arrival(l_at + i).wait_recv()
     for b in range(2):
-        l_copy(b).start()
+        lp_copy(0, b).start()
+        lx_copy(b).start()
+    relays(32, 38)
+    x_arrival(4).wait_recv()
+    p_copy(3).start()
+    relays(38, 42)
+    for b in range(2):
+        lx_copy(b).wait_recv()
+        lp_copy(1, b).start()
     relay(42)
     p_arrival(3).wait_recv()
     second_factor(2)
     relay(43)
     second_factor(3)
-    relay(44)
+    relays(44, 46)
     for b in range(2):
-        l_copy(b).wait_recv()
-        for at, block in ((core, lane[b, pl.ds(l_at, n_l)]), (1 - core, l10p[b])):
-            h, l = split(block.reshape(half, CW))
-            lh[at, pl.ds(b * half, half)] = h
-            ll[at, pl.ds(b * half, half)] = l
+        lp_copy(0, b).wait_recv()
+        lp_copy(1, b).wait_recv()
+        for at, e, block in ((core, x, lane[b, pl.ds(l_at, n_l)]), (core, 1 - x, l10x[b]),
+                             (1 - core, x, l10p[0, b]), (1 - core, 1 - x, l10p[1, b])):
+            h, l = split(block.reshape(quarter, CW))
+            rows = pl.ds(pl.multiple_of(b * half + e * quarter, quarter), quarter)
+            lh[at, rows] = h
+            ll[at, rows] = l
     load_rest.wait()
     for t in range(4):
-        relay(45 + 2 * t)
+        relay(46 + t)
         first_factor(t)
-        relay(46 + 2 * t)
 
     def gather(g):
-        k, h = g // 2, g % 2
-        start = k * ppc + jnp.where(k >= 2, n_l, 0) + h * n_l
-
-        @pl.loop(start, start + n_l)
+        start = g * n_h + jnp.where(g >= 3, n_l, 0)
+
+        @pl.loop(start, start + n_h)
         def _(p):
             y_arrival(p).wait_recv()
 
         for b in range(2):
             rows = slice(b * half, (b + 1) * half)
-            xh[rows], xl[rows] = split(lane[b, pl.ds(start, n_l)].reshape(half, CW))
+            xh[rows], xl[rows] = split(lane[b, pl.ds(start, n_h)].reshape(half, CW))
 
     def update(g, t):
         k, h = g // 2, g % 2
@@ -280,11 +311,7 @@
 
         @pl.when(jnp.logical_and(g < 6, t < 3))
         def _():
-            relay(53 + 3 * g + t)
-
-        @pl.when(n == 24)
-        def _():
-            relays(71, n_piece)
+            relay(50 + 3 * g + t)
 
         @pl.when(t == 0)
         def _():
@@ -292,24 +319,28 @@
 
         update(g, t)
 
-    x_copy(0).wait_send()
-    x_copy(1).wait_send()
+    for i in range(5):
+        x_copy(i).wait_send()
     for i in range(4):
         p_copy(i).wait_send()
     for b in range(2):
-        l_copy(b).wait_send()
+        lx_copy(b).wait_send()
+        lp_copy(0, b).wait_send()
+        lp_copy(1, b).wait_send()
 
     @pl.when(r == 1)
     def _():
         for i in range(n_l):
             t_copy(i).wait_send()
 
-    @pl.loop(jnp.where(z == 0, n_piece - WINDOW, 0), n_piece)
+    @pl.loop(jnp.where(z == 0, n_piece - Y_WINDOW, 0), n_piece)
     def _(p):
         y_copy(p).wait_send()
 
-        @pl.when(has_up)
-        def _():
+    @pl.when(has_up)
+    def _():
+        @pl.loop(jnp.where(z == 0, n_piece - Z_WINDOW, 0), n_piece)
+        def _(p):
             z_copy(p).wait_send()
 
 
@@ -317,7 +348,7 @@
     nb = rhs.shape[1]
     n_chunk = rhs.shape[2] // CW
     ppc = nb // PR
-    n_l = ppc // 2
+    n_l = ppc // 4
     n_piece = n_chunk * ppc + n_l
     f32, bf16, dma = jnp.float32, jnp.bfloat16, pltpu.SemaphoreType.DMA
     anywhere = pl.BlockSpec(memory_space=pl.ANY)
@@ -329,6 +360,7 @@
         scratch_shapes=[
             pltpu.VMEM((2, n_piece, PR, CW), f32),
             pltpu.VMEM((4, 2, nb, CW), f32),
+            pltpu.VMEM((2, 2, n_l, PR, CW), f32),
             pltpu.VMEM((2, n_l, PR, CW), f32),
             pltpu.VMEM((2, nb, nb), f32),
             pltpu.VMEM((2 * nb, 2 * nb), bf16),
@@ -341,8 +373,8 @@
             pltpu.VMEM((nb, CW), bf16),
             dma((n_chunk + 1,)), dma((2,)), dma((2,)),
             dma((n_piece,)), dma((n_piece,)), dma((n_piece,)), dma((n_piece,)),
-            dma((2,)), dma((2,)), dma((4,)), dma((4,)),
-            dma((n_l,)), dma((n_l,)), dma((2,)), dma((2,)),
+            dma((5,)), dma((5,)), dma((4,)), dma((4,)),
+            dma((n_l,)), dma((n_l,)), dma((2, 2)), dma((2, 2)), dma((2,)), dma((2,)),
         ],
         compiler_params=pltpu.CompilerParams(
             collective_id=0, has_side_effects=True, vmem_limit_bytes=59 * 1024 * 1024),

time: 76.7 us -> 69.1 us (0.901)
  Pallas kernels: 74.5 us -> 66.8 us
    pallas_call x1, Pallas kernels: 74.5 us -> 66.8 us  [shards(): pl.pallas_call(functools.partial(kernel, n_row), out_shape=pltpu.VMEM(rhs...]
where the time goes in v4:
time: 69.1 us; the launch traced here: 68.8 us
  Pallas kernels  66.8 us (97%)
  local copies, waits for them, and re-layouts  2.02 us (3%)
    pallas_call x1, Pallas kernels, shards(): pl.pallas_call(functools.partial(kernel, n_row), out_shape=pltpu.VMEM(rhs...  66.8 us
    unnamed x1, local copies, waits for them, and re-layouts  2.02 us

profile of v4, /device:TPU:28, one launch (start us, length us, event | category | flops | bytes accessed | tf_op | source)
XLA Modules:
  0.0 68.8 jit_solution(4050251199439552129)
XLA Ops:
  0.0 66.8 %shard_map.37 = f32[2,512,1024]{2,1,0:T(8,128)S(1)} custom-call(f32[2,512,1024]{2,1,0:T(8,128)} %rhs.1, f32[2,512,256]{2,1,0:T(8,128)} %fac.1, f32[2,512,512]{2,1,0:T(8,128)} %inv.1), custom_call_target="tpu_custom_call" | custom-call | flops 8000000000 | bytes 12582912 | tf_op jit(solution)/shard_map/pallas_call | solution.py:355
  66.8 2.0 %copy.5 = f32[2,512,1024]{2,1,0:T(8,128)} copy(f32[2,512,1024]{2,1,0:T(8,128)S(1)} %shard_map.37) | data formatting | bytes 8388608

commit v5 on v4

--- a/solution.py
+++ b/solution.py
@@ -35,7 +35,7 @@
     n_h = ppc // 2
     n_l = ppc // 4
     n_piece = n_chunk * ppc + n_l
-    l_at = 3 * n_h
+    l_at = 2 * n_h
     half, quarter = nb // 2, nb // 4
 
     r = lax.axis_index("row")
@@ -76,7 +76,7 @@
         pl.semaphore_signal(barrier, inc=1, device_id=down, device_id_type=MESH)
 
     def first_piece(g):
-        return g * n_h + (n_l if g >= 3 else 0)
+        return g * n_h + (n_l if g >= 2 else 0)
 
     def fill(k):
         load_lead(k).wait()
@@ -104,25 +104,26 @@
         return remote(lane.at[1 - y, p], lane.at[1 - y, p], ys.at[p], yr.at[p], across)
 
     def x_ref(ref, at, i):
-        part = ref.at[0] if i < 4 else ref.at[1]
-        if at is not None:
-            part = ref.at[at, 0] if i < 4 else ref.at[at, 1]
-        return part.at[pl.ds((1, 3, 0, 2)[i] * quarter, quarter)] if i < 4 else part
+        rows = pl.ds((1, 3, 0, 2)[i] * quarter, quarter) if i < 4 else pl.ds((i - 4) * half, half)
+        return ref.at[i // 4, rows] if at is None else ref.at[at, i // 4, rows]
 
     def x_copy(i):
         return remote(x_ref(fac, None, i), x_ref(pan, c, i), xs.at[i], xr.at[i], far)
 
     def x_arrival(i):
         return remote(x_ref(fac, None, i), x_ref(pan, peer, i), xs.at[i], xr.at[i], far)
+
+    def p_ref(at, i):
+        return pan.at[at, i % 2] if i < 3 else pan.at[at, 1, pl.ds((i - 3) * half, half)]
 
     def p_copy(i):
         if i < 2:
             return remote(fac.at[i], pan.at[c, i], ps.at[i], pr.at[i], beside)
-        return remote(pan.at[peer, i - 2], pan.at[peer, i - 2], ps.at[i], pr.at[i], beside)
+        return remote(p_ref(peer, i), p_ref(peer, i), ps.at[i], pr.at[i], beside)
 
     def p_arrival(i):
         at = partner if i < 2 else peer2
-        return remote(pan.at[at, i % 2], pan.at[at, i % 2], ps.at[i], pr.at[i], beside)
+        return remote(p_ref(at, i), p_ref(at, i), ps.at[i], pr.at[i], beside)
 
     def t_copy(i):
         rows = pl.ds(pl.multiple_of(x * quarter + i * PR, PR), PR)
@@ -175,38 +176,52 @@
     relay(7)
     x_copy(2).start()
     x_copy(3).start()
-    for i in range(2):
-        inv_copy[i].wait()
-        for h in range(2):
-            rows = slice(h * half, (h + 1) * half)
-            ih[i, rows], il[i, rows] = split(invf[i, rows])
-            relay(8 + 2 * i + h)
-        if i == 0:
-            x_arrival(0).wait_recv()
-            x_arrival(1).wait_recv()
-            for copy in own:
-                copy.wait()
-
-            @pl.when(r == 1)
-            def _():
-                for e in range(n_l):
-                    t_copy(e).start()
-                rows = pl.ds(pl.multiple_of(half + x * quarter, quarter), quarter)
-                lane[1, pl.ds(l_at, n_l)] = pan[core, 0, rows].reshape(n_l, PR, CW)
-
-    relays(12, 16)
+
+    def split_inverse(i, h):
+        rows = slice(h * half, (h + 1) * half)
+        ih[i, rows], il[i, rows] = split(invf[i, rows])
+
+    inv_copy[0].wait()
+    split_inverse(0, 0)
+    relay(8)
+    x_arrival(0).wait_recv()
+    x_arrival(1).wait_recv()
+    for copy in own:
+        copy.wait()
+
+    @pl.when(r == 1)
+    def _():
+        for e in range(n_l):
+            t_copy(e).start()
+        rows = pl.ds(pl.multiple_of(half + x * quarter, quarter), quarter)
+        lane[1, pl.ds(l_at, n_l)] = pan[core, 0, rows].reshape(n_l, PR, CW)
+
+    relay(9)
+    split_inverse(0, 1)
+    relay(10)
+    inv_copy[1].wait()
+    split_inverse(1, 0)
+    relay(11)
+    split_inverse(1, 1)
+    relay(12)
     x_copy(4).start()
+    relays(13, 16)
+
+    @pl.when(r == 0)
+    def _():
+        for i in range(n_l):
+            t_copy(i).wait_recv()
+
     relays(16, 19)
     x_arrival(2).wait_recv()
     x_arrival(3).wait_recv()
     p_copy(2).start()
     relays(19, 24)
-
-    @pl.when(r == 0)
-    def _():
-        for i in range(n_l):
-            t_copy(i).wait_recv()
-
+    for i in range(n_l):
+        y_arrival(l_at + i).wait_recv()
+    for b in range(2):
+        lp_copy(0, b).start()
+        lx_copy(b).start()
     relays(24, 26)
     for i in range(3):
         p_arrival(i).wait_recv()
@@ -254,25 +269,19 @@
     second_factor(0)
     relay(26)
     second_factor(1)
-    relays(27, 32)
-    for i in range(n_l):
-        y_arrival(l_at + i).wait_recv()
-    for b in range(2):
-        lp_copy(0, b).start()
-        lx_copy(b).start()
-    relays(32, 38)
+    relay(27)
     x_arrival(4).wait_recv()
     p_copy(3).start()
-    relays(38, 42)
+    relay(28)
+    x_copy(5).start()
+    relays(29, 33)
+    p_arrival(3).wait_recv()
+    second_factor(2)
+    relays(33, 36)
     for b in range(2):
         lx_copy(b).wait_recv()
         lp_copy(1, b).start()
-    relay(42)
-    p_arrival(3).wait_recv()
-    second_factor(2)
-    relay(43)
-    second_factor(3)
-    relays(44, 46)
+    relays(36, 39)
     for b in range(2):
         lp_copy(0, b).wait_recv()
         lp_copy(1, b).wait_recv()
@@ -283,12 +292,20 @@
             lh[at, rows] = h
             ll[at, rows] = l
     load_rest.wait()
-    for t in range(4):
-        relay(46 + t)
+    for t in range(3):
+        relay(39 + t)
         first_factor(t)
+    relay(42)
+    x_arrival(5).wait_recv()
+    p_copy(4).start()
+    relays(43, 46)
+    p_arrival(4).wait_recv()
+    second_factor(3)
+    relay(46)
+    first_factor(3)
 
     def gather(g):
-        start = g * n_h + jnp.where(g >= 3, n_l, 0)
+        start = g * n_h + jnp.where(g >= 2, n_l, 0)
 
         @pl.loop(start, start + n_h)
         def _(p):
@@ -309,9 +326,9 @@
     def _(n):
         g, t = n // 4, n % 4
 
-        @pl.when(jnp.logical_and(g < 6, t < 3))
-        def _():
-            relay(50 + 3 * g + t)
+        @pl.when(jnp.logical_and(g < 6, n % 8 < 7))
+        def _():
+            relay(47 + n - n // 8)
 
         @pl.when(t == 0)
         def _():
@@ -319,9 +336,9 @@
 
         update(g, t)
 
+    for i in range(6):
+        x_copy(i).wait_send()
     for i in range(5):
-        x_copy(i).wait_send()
-    for i in range(4):
         p_copy(i).wait_send()
     for b in range(2):
         lx_copy(b).wait_send()
@@ -373,7 +390,7 @@
             pltpu.VMEM((nb, CW), bf16),
             dma((n_chunk + 1,)), dma((2,)), dma((2,)),
             dma((n_piece,)), dma((n_piece,)), dma((n_piece,)), dma((n_piece,)),
-            dma((5,)), dma((5,)), dma((4,)), dma((4,)),
+            dma((6,)), dma((6,)), dma((5,)), dma((5,)),
             dma((n_l,)), dma((n_l,)), dma((2, 2)), dma((2, 2)), dma((2,)), dma((2,)),
         ],
         compiler_params=pltpu.CompilerParams(

time: 69.1 us -> 69.8 us (1.010)
  Pallas kernels: 66.8 us -> 67.7 us
    pallas_call x1, Pallas kernels: 66.8 us -> 67.7 us  [shards(): pl.pallas_call(functools.partial(kernel, n_row), out_shape=pltpu.VMEM(rhs...]
where the time goes in v5:
time: 69.8 us; the launch traced here: 69.7 us
  Pallas kernels  67.7 us (97%)
  local copies, waits for them, and re-layouts  2.02 us (3%)
    pallas_call x1, Pallas kernels, shards(): pl.pallas_call(functools.partial(kernel, n_row), out_shape=pltpu.VMEM(rhs...  67.7 us
    unnamed x1, local copies, waits for them, and re-layouts  2.02 us

profile of v5, /device:TPU:28, one launch (start us, length us, event | category | flops | bytes accessed | tf_op | source)
XLA Modules:
  0.0 69.7 jit_solution(8747560444804089654)
XLA Ops:
  0.0 67.7 %shard_map.37 = f32[2,512,1024]{2,1,0:T(8,128)S(1)} custom-call(f32[2,512,1024]{2,1,0:T(8,128)} %rhs.1, f32[2,512,256]{2,1,0:T(8,128)} %fac.1, f32[2,512,512]{2,1,0:T(8,128)} %inv.1), custom_call_target="tpu_custom_call" | custom-call | flops 8000000000 | bytes 12582912 | tf_op jit(solution)/shard_map/pallas_call | solution.py:372
  67.7 2.0 %copy.5 = f32[2,512,1024]{2,1,0:T(8,128)} copy(f32[2,512,1024]{2,1,0:T(8,128)S(1)} %shard_map.37) | data formatting | bytes 8388608

commit v6 on v5

--- a/solution.py
+++ b/solution.py
@@ -245,11 +245,20 @@
                  + dot3(bh, bl, ih[i, half:, :half], il[i, half:, :half]))
         return first, dot3(bh, bl, ih[i, half:, half:], il[i, half:, half:])
 
+    def columns(e, b):
+        return slice((2 * e + b) * quarter, (2 * e + b + 1) * quarter)
+
     def keep(t, b, products):
         rows = slice(t * half, (t + 1) * half)
         for h, value in enumerate(products):
-            at = slice((2 * h + b) * CW, (2 * h + b + 1) * CW)
-            mh[rows, at], ml[rows, at] = split(value)
+            high, low = split(value)
+            for e in range(2):
+                part = slice(e * quarter, (e + 1) * quarter)
+                mh[rows, columns(2 * h + e, b)] = high[:, part]
+                ml[rows, columns(2 * h + e, b)] = low[:, part]
+
+    def kept(ref, rows, h):
+        return jnp.concatenate([ref[rows, columns(2 * h, 1)], ref[rows, columns(2 * h + 1, 1)]], axis=1)
 
     def second_factor(t):
         keep(t, 1, triangle(1, [split(panel(2, t)), split(panel(3, t))]))
@@ -260,9 +269,8 @@
         for q in range(2):
             value = panel(q, t)
             for h in range(2):
-                at = slice((2 * h + 1) * CW, (2 * h + 2) * CW)
                 ks = slice(h * half, (h + 1) * half)
-                value = value - dot3(mh[rows, at], ml[rows, at], lh[q, ks], ll[q, ks])
+                value = value - dot3(kept(mh, rows, h), kept(ml, rows, h), lh[q, ks], ll[q, ks])
             parts.append(split(value))
         keep(t, 0, triangle(0, parts))
 
@@ -304,37 +312,45 @@
     relay(46)
     first_factor(3)
 
-    def gather(g):
-        start = g * n_h + jnp.where(g >= 2, n_l, 0)
-
-        @pl.loop(start, start + n_h)
+    def gather(start, quarters):
+        count = n_h // 2
+
+        @pl.loop(start, start + quarters * count)
         def _(p):
             y_arrival(p).wait_recv()
 
-        for b in range(2):
-            rows = slice(b * half, (b + 1) * half)
-            xh[rows], xl[rows] = split(lane[b, pl.ds(start, n_h)].reshape(half, CW))
-
-    def update(g, t):
-        k, h = g // 2, g % 2
+        for e in range(quarters):
+            for b in range(2):
+                rows = slice((2 * e + b) * quarter, (2 * e + b + 1) * quarter)
+                xh[rows], xl[rows] = split(lane[b, pl.ds(start + e * count, count)].reshape(quarter, CW))
+
+    def update(k, t, ks, width):
         rows = pl.ds(pl.multiple_of(t * half, half), half)
         place = (t // 2, pl.ds(pl.multiple_of((t % 2) * half, half), half), pl.ds(pl.multiple_of(k * CW, CW), CW))
-        ks = pl.ds(pl.multiple_of(h * 2 * CW, 2 * CW), 2 * CW)
-        out[place] = out[place] - dot3(mh[rows, ks], ml[rows, ks], xh[...], xl[...])
-
-    @pl.loop(0, 4 * 2 * n_chunk)
+        out[place] = out[place] - dot3(mh[rows, ks], ml[rows, ks], xh[:width], xl[:width])
+
+    last = 2 * n_chunk - 1
+
+    @pl.loop(0, 4 * last)
     def _(n):
         g, t = n // 4, n % 4
 
-        @pl.when(jnp.logical_and(g < 6, n % 8 < 7))
-        def _():
-            relay(47 + n - n // 8)
+        @pl.when(t < 3)
+        def _():
+            relay(47 + 3 * g + t)
 
         @pl.when(t == 0)
         def _():
-            gather(g)
-
-        update(g, t)
+            gather(g * n_h + jnp.where(g >= 2, n_l, 0), 2)
+
+        update(g // 2, t, pl.ds(pl.multiple_of((g % 2) * nb, nb), nb), nb)
+
+    for e in range(2):
+        gather(first_piece(last) + e * (n_h // 2), 1)
+
+        @pl.loop(0, 4)
+        def _(t):
+            update(n_chunk - 1, t, pl.ds(nb + e * half, half), half)
 
     for i in range(6):
         x_copy(i).wait_send()

time: 69.8 us -> 69.3 us (level)
  no operation moved by 1% of the time
where the time goes in v6:
time: 69.3 us; the launch traced here: 69.2 us
  Pallas kernels  67.1 us (97%)
  local copies, waits for them, and re-layouts  2.02 us (3%)
    pallas_call x1, Pallas kernels, shards(): pl.pallas_call(functools.partial(kernel, n_row), out_shape=pltpu.VMEM(rhs...  67.1 us
    unnamed x1, local copies, waits for them, and re-layouts  2.02 us

profile of v6, /device:TPU:28, one launch (start us, length us, event | category | flops | bytes accessed | tf_op | source)
XLA Modules:
  0.0 69.2 jit_solution(12443233196841826411)
XLA Ops:
  0.0 67.1 %shard_map.37 = f32[2,512,1024]{2,1,0:T(8,128)S(1)} custom-call(f32[2,512,1024]{2,1,0:T(8,128)} %rhs.1, f32[2,512,256]{2,1,0:T(8,128)} %fac.1, f32[2,512,512]{2,1,0:T(8,128)} %inv.1), custom_call_target="tpu_custom_call" | custom-call | flops 8000000000 | bytes 12582912 | tf_op jit(solution)/shard_map/pallas_call | solution.py:388
  67.1 2.0 %copy.5 = f32[2,512,1024]{2,1,0:T(8,128)} copy(f32[2,512,1024]{2,1,0:T(8,128)S(1)} %shard_map.37) | data formatting | bytes 8388608

commit v7 on v6

--- a/solution.py
+++ b/solution.py
@@ -212,17 +212,18 @@
         for i in range(n_l):
             t_copy(i).wait_recv()
 
-    relays(16, 19)
+    relays(16, 22)
     x_arrival(2).wait_recv()
     x_arrival(3).wait_recv()
     p_copy(2).start()
-    relays(19, 24)
+    relays(22, 24)
     for i in range(n_l):
         y_arrival(l_at + i).wait_recv()
     for b in range(2):
         lp_copy(0, b).start()
         lx_copy(b).start()
-    relays(24, 26)
+    x_copy(5).start()
+    relays(24, 29)
     for i in range(3):
         p_arrival(i).wait_recv()
 
@@ -275,21 +276,19 @@
         keep(t, 0, triangle(0, parts))
 
     second_factor(0)
-    relay(26)
+    relay(29)
     second_factor(1)
-    relay(27)
+    relays(30, 32)
     x_arrival(4).wait_recv()
     p_copy(3).start()
-    relay(28)
-    x_copy(5).start()
-    relays(29, 33)
+    relays(32, 36)
     p_arrival(3).wait_recv()
     second_factor(2)
-    relays(33, 36)
+    relays(36, 38)
     for b in range(2):
         lx_copy(b).wait_recv()
         lp_copy(1, b).start()
-    relays(36, 39)
+    relays(38, 41)
     for b in range(2):
         lp_copy(0, b).wait_recv()
         lp_copy(1, b).wait_recv()
@@ -301,15 +300,15 @@
             ll[at, rows] = l
     load_rest.wait()
     for t in range(3):
-        relay(39 + t)
+        relay(41 + t)
         first_factor(t)
-    relay(42)
+    relays(44, 46)
     x_arrival(5).wait_recv()
     p_copy(4).start()
-    relays(43, 46)
+    relays(46, 49)
     p_arrival(4).wait_recv()
     second_factor(3)
-    relay(46)
+    relay(49)
     first_factor(3)
 
     def gather(start, quarters):
@@ -335,9 +334,9 @@
     def _(n):
         g, t = n // 4, n % 4
 
-        @pl.when(t < 3)
-        def _():
-            relay(47 + 3 * g + t)
+        @pl.when(t < jnp.where(g < 4, 3, 2))
+        def _():
+            relay(50 + 3 * g - jnp.maximum(g - 4, 0) + t)
 
         @pl.when(t == 0)
         def _():

time: 69.3 us -> 69.5 us (level)
  no operation moved by 1% of the time
where the time goes in v7:
time: 69.5 us; the launch traced here: 69.3 us
  Pallas kernels  67.3 us (97%)
  local copies, waits for them, and re-layouts  2.02 us (3%)
    pallas_call x1, Pallas kernels, shards(): pl.pallas_call(functools.partial(kernel, n_row), out_shape=pltpu.VMEM(rhs...  67.3 us
    unnamed x1, local copies, waits for them, and re-layouts  2.02 us

profile of v7, /device:TPU:28, one launch (start us, length us, event | category | flops | bytes accessed | tf_op | source)
XLA Modules:
  0.0 69.3 jit_solution(6312049391802571600)
XLA Ops:
  0.0 67.3 %shard_map.37 = f32[2,512,1024]{2,1,0:T(8,128)S(1)} custom-call(f32[2,512,1024]{2,1,0:T(8,128)} %rhs.1, f32[2,512,256]{2,1,0:T(8,128)} %fac.1, f32[2,512,512]{2,1,0:T(8,128)} %inv.1), custom_call_target="tpu_custom_call" | custom-call | flops 8000000000 | bytes 12582912 | tf_op jit(solution)/shard_map/pallas_call | solution.py:387
  67.3 2.0 %copy.5 = f32[2,512,1024]{2,1,0:T(8,128)} copy(f32[2,512,1024]{2,1,0:T(8,128)S(1)} %shard_map.37) | data formatting | bytes 8388608

commit v8 on v6

--- a/solution.py
+++ b/solution.py
@@ -28,7 +28,8 @@
 
 
 def kernel(n_row, rhs, fac, inv, out, lane, pan, l10p, l10x, invf, mh, ml, ih, il, lh, ll, xh, xl,
-           acc_sem, inv_sem, own_sem, zs, zr, ys, yr, xs, xr, ps, pr, ts, tr, ls, lr, us, ur):
+           acc_sem, inv_sem, own_sem, zs, zr, ys, yr, xs, xr, ps, pr, ts, tr, ls, lr, us, ur,
+           zs2, zr2, ys2, yr2):
     nb = rhs.shape[1]
     n_chunk = rhs.shape[2] // CW
     ppc = nb // PR
@@ -36,6 +37,7 @@
     n_l = ppc // 4
     n_piece = n_chunk * ppc + n_l
     l_at = 2 * n_h
+    n_main = n_piece - n_h
     half, quarter = nb // 2, nb // 4
 
     r = lax.axis_index("row")
@@ -154,6 +156,29 @@
             y_copy(p - Y_WINDOW).wait_send()
 
         y_copy(p).start()
+
+    def fine(b, i):
+        return lane.at[b, n_main + i // 2, pl.ds(pl.multiple_of((i % 2) * (PR // 2), PR // 2), PR // 2)]
+
+    def z_fine(i):
+        return remote(fine(y, i), fine(y, i), zs2.at[i], zr2.at[i], up)
+
+    def y_fine(i):
+        return remote(fine(y, i), fine(y, i), ys2.at[i], yr2.at[i], across)
+
+    def y_fine_arrival(i):
+        return remote(fine(1 - y, i), fine(1 - y, i), ys2.at[i], yr2.at[i], across)
+
+    def relay_fine(i):
+        @pl.when(has_down)
+        def _():
+            z_fine(i).wait_recv()
+
+        @pl.when(has_up)
+        def _():
+            z_fine(i).start()
+
+        y_fine(i).start()
 
     def relays(start, stop):
         @pl.loop(start, stop)
@@ -315,10 +340,6 @@
     def gather(start, quarters):
         count = n_h // 2
 
-        @pl.loop(start, start + quarters * count)
-        def _(p):
-            y_arrival(p).wait_recv()
-
         for e in range(quarters):
             for b in range(2):
                 rows = slice((2 * e + b) * quarter, (2 * e + b + 1) * quarter)
@@ -335,17 +356,33 @@
     def _(n):
         g, t = n // 4, n % 4
 
-        @pl.when(t < 3)
-        def _():
-            relay(47 + 3 * g + t)
+        @pl.when(n < 13)
+        def _():
+            relay(47 + n)
+
+        @pl.when(n >= 13)
+        def _():
+            relay_fine(n - 13)
 
         @pl.when(t == 0)
         def _():
-            gather(g * n_h + jnp.where(g >= 2, n_l, 0), 2)
+            start = g * n_h + jnp.where(g >= 2, n_l, 0)
+
+            @pl.loop(start, start + n_h)
+            def _(p):
+                y_arrival(p).wait_recv()
+
+            gather(start, 2)
 
         update(g // 2, t, pl.ds(pl.multiple_of((g % 2) * nb, nb), nb), nb)
 
+    relay_fine(15)
+
     for e in range(2):
+        @pl.loop(e * n_h, (e + 1) * n_h)
+        def _(i):
+            y_fine_arrival(i).wait_recv()
+
         gather(first_piece(last) + e * (n_h // 2), 1)
 
         @pl.loop(0, 4)
@@ -366,15 +403,23 @@
         for i in range(n_l):
             t_copy(i).wait_send()
 
-    @pl.loop(jnp.where(z == 0, n_piece - Y_WINDOW, 0), n_piece)
+    @pl.loop(jnp.where(z == 0, n_main - Y_WINDOW, 0), n_main)
     def _(p):
         y_copy(p).wait_send()
 
+    @pl.loop(0, 2 * n_h)
+    def _(i):
+        y_fine(i).wait_send()
+
     @pl.when(has_up)
     def _():
-        @pl.loop(jnp.where(z == 0, n_piece - Z_WINDOW, 0), n_piece)
+        @pl.loop(jnp.where(z == 0, n_main - Z_WINDOW, 0), n_main)
         def _(p):
             z_copy(p).wait_send()
+
+        @pl.loop(0, 2 * n_h)
+        def _(i):
+            z_fine(i).wait_send()
 
 
 def shards(n_row, rhs, factor, inverses):
@@ -408,6 +453,7 @@
             dma((n_piece,)), dma((n_piece,)), dma((n_piece,)), dma((n_piece,)),
             dma((6,)), dma((6,)), dma((5,)), dma((5,)),
             dma((n_l,)), dma((n_l,)), dma((2, 2)), dma((2, 2)), dma((2,)), dma((2,)),
+            dma((ppc,)), dma((ppc,)), dma((ppc,)), dma((ppc,)),
         ],
         compiler_params=pltpu.CompilerParams(
             collective_id=0, has_side_effects=True, vmem_limit_bytes=59 * 1024 * 1024),

time: 69.3 us -> 71.1 us (1.026)
  Pallas kernels: 67.1 us -> 68.9 us
    pallas_call x1, Pallas kernels: 67.1 us -> 68.9 us  [shards(): pl.pallas_call(functools.partial(kernel, n_row), out_shape=pltpu.VMEM(rhs...]
where the time goes in v8:
time: 71.1 us; the launch traced here: 70.9 us
  Pallas kernels  68.9 us (97%)
  local copies, waits for them, and re-layouts  2.02 us (3%)
    pallas_call x1, Pallas kernels, shards(): pl.pallas_call(functools.partial(kernel, n_row), out_shape=pltpu.VMEM(rhs...  68.9 us
    unnamed x1, local copies, waits for them, and re-layouts  2.02 us

profile of v8, /device:TPU:28, one launch (start us, length us, event | category | flops | bytes accessed | tf_op | source)
XLA Modules:
  0.0 70.9 jit_solution(17366352509039160889)
XLA Ops:
  0.0 68.9 %shard_map.37 = f32[2,512,1024]{2,1,0:T(8,128)S(1)} custom-call(f32[2,512,1024]{2,1,0:T(8,128)} %rhs.1, f32[2,512,256]{2,1,0:T(8,128)} %fac.1, f32[2,512,512]{2,1,0:T(8,128)} %inv.1), custom_call_target="tpu_custom_call" | custom-call | flops 8000000000 | bytes 12582912 | tf_op jit(solution)/shard_map/pallas_call | solution.py:433
  68.9 2.0 %copy.5 = f32[2,512,1024]{2,1,0:T(8,128)} copy(f32[2,512,1024]{2,1,0:T(8,128)S(1)} %shard_map.37) | data formatting | bytes 8388608
